TPU v7x, 512 devices: a whole 4x4x16 slice. The times are simulated.
512 devices in a mesh: dp: 8 (over y, core), node: 64 (over z, x).
Axes of the slice: x: 4, y: 4, z: 16, core: 2. Of those that a mesh axis runs over, the one named last changes fastest.
Arguments:
- leaf_logp: float32 [128, 32, 1024], P('node', None, 'dp'), may hold values from -108 to 0, as said below
- weights: bfloat16 [128, 32, 1024], P('node'), may hold values from 0.0099487305 to 1
- upper_flows: float32 [128, 32, 1024], P('node', None, 'dp'), may hold values from 0.01 to 1
- leaf_asks: int32 [64, 64], P('node'), may hold values from 0 to 1
- prod_asks: int32 [64, 64], P('node'), may hold values from 0 to 1
- prod_child: int32 [128, 8], P('node'), may hold values from 0 to 63
- prod_valid: int32 [128, 8], P('node'), may hold values 0 or 1
- sum_child: int32 [128, 32], P('node'), may hold values from 0 to 63
- sum_valid: int32 [128, 32], P('node'), may hold values from 0 to 1, as said below
Outputs:
- sum_loglik: float32 [128, 32, 1024], P('node', None, 'dp')
- weight_flows: float32 [128, 32, 1024], P('node', None, 'dp')
- prod_flows: float32 [128, 32, 1024], P('node', None, 'dp')
Inputs may be any that keep to these rules, and one draw needn't show every extreme that they name: `leaf_logp`: log-probabilities, so no entry is positive. `leaf_asks`: entry (d, o) is which of owner o's 2 blocks device d reads. `prod_asks`: entry (d, o) is which of owner o's 2 blocks device d reads. `sum_valid`: the first child slot of every sum block is valid.
All inputs are finite; a program needn't handle non-finite values. No bound on the sum of `prod_valid` on one device may be relied on, other than what follows from the above.
Results may differ from a plain program's by a relative error of at most 0.0022.
Values sent between devices are 32-bit elements; how exact they have to be, the bound alone decides.
A program may use at most 64 MiB of HBM per device.

v0:
```python
import jax
import jax.numpy as jnp
from jax import lax
from jax.sharding import PartitionSpec as P


def local(
    leaf_logp,
    weights,
    upper_flows,
    leaf_asks,
    prod_asks,
    prod_child,
    prod_valid,
    sum_child,
    sum_valid,
):
    block_count, node_width, tok_count = leaf_logp.shape
    owners = lax.axis_size("node")
    slot_iota = jnp.arange(owners, dtype=jnp.int32)
    block_iota = jnp.arange(block_count, dtype=jnp.int32)
    exact = lax.Precision.HIGHEST
    asked = (
        lax.all_to_all(
            leaf_asks.reshape(owners, 1), "node", split_axis=0, concat_axis=0, tiled=True
        ),
        lax.all_to_all(
            prod_asks.reshape(owners, 1), "node", split_axis=0, concat_axis=0, tiled=True
        ),
    )
    ask_rows = (leaf_asks[0], prod_asks[0])

    def fetch_blocks(layer_vals, which_ask):
        whole_layer = lax.all_gather(layer_vals, "node", axis=0, tiled=True)
        return whole_layer[slot_iota * block_count + ask_rows[which_ask]]

    leaf_slots = fetch_blocks(leaf_logp, 0)
    mix_count = jnp.sum(
        (prod_child[:, :, None] == slot_iota[None, None, :]) * prod_valid[:, :, None], axis=1
    ).astype(jnp.float32)
    products = jnp.einsum("bo,okt->bkt", mix_count, leaf_slots, precision=exact)
    prod_slots = fetch_blocks(products, 1)
    picked = prod_slots[sum_child]
    is_valid = (sum_valid > 0)[:, :, None, None]
    col_max = jnp.max(jnp.where(is_valid, picked, -jnp.inf), axis=(1, 2))
    scaled = jnp.where(is_valid, jnp.exp(picked - col_max[:, None, None, :]), 0.0).astype(
        jnp.bfloat16
    )
    edges = picked.shape[1]
    flat_rows = scaled.reshape(block_count, edges * node_width, tok_count)
    totals = jnp.einsum("bkj,bjt->bkt", weights, flat_rows, preferred_element_type=jnp.float32)
    sum_loglik = jnp.log(totals) + col_max[:, None, :]
    ratios = (upper_flows / totals).astype(jnp.bfloat16)
    partial_counts = jnp.einsum(
        "bkt,bjt->bkj", ratios, flat_rows, preferred_element_type=jnp.float32
    )
    summed_counts = lax.psum_scatter(partial_counts, "dp", scatter_dimension=2, tiled=True)
    share_cols = summed_counts.shape[2]
    col_start = lax.axis_index("dp") * share_cols
    weight_cols = lax.dynamic_slice_in_dim(weights, col_start, share_cols, 2).astype(jnp.float32)
    weight_flows = weight_cols * summed_counts / (tok_count * lax.axis_size("dp"))
    spread_back = jnp.einsum("bkj,bkt->bjt", weights, ratios, preferred_element_type=jnp.float32)
    child_flows = (flat_rows.astype(jnp.float32) * spread_back).reshape(
        block_count, edges, node_width, tok_count
    )
    routing = (sum_child[:, :, None] == slot_iota[None, None, :]).astype(jnp.float32)
    slot_flows = jnp.einsum("beo,bekt->okt", routing, child_flows, precision=exact)
    returned = lax.all_to_all(slot_flows, "node", split_axis=0, concat_axis=0, tiled=True)
    pick_block = (asked[1][:, 0][:, None] == block_iota[None, :]).astype(jnp.float32)
    prod_flows = jnp.einsum("cb,ckt->bkt", pick_block, returned, precision=exact)
    return (sum_loglik, weight_flows, prod_flows)


def solution(mesh):
    in_specs = (
        P("node", None, "dp"),
        P("node", None, None),
        P("node", None, "dp"),
        P("node", None),
        P("node", None),
        P("node", None),
        P("node", None),
        P("node", None),
        P("node", None),
    )
    out_specs = (P("node", None, "dp"), P("node", None, "dp"), P("node", None, "dp"))
    return jax.shard_map(local, mesh=mesh, in_specs=in_specs, out_specs=out_specs, check_vma=False)
```

profile of v0, /device:TPU:2, one launch (start us, length us, event | category | flops | bytes accessed | tf_op | source)
XLA Modules:
  0.0 369.7 jit_solution(18280250931427675096)
XLA Ops:
  7.2 0.7 all-gather.3.cloned.1.call-update
  8.0 0.7 fusion.14
  8.6 0.8 select_reduce_fusion.1
  9.4 145.9 %all-gather.3.cloned.1.call-done = f32[128,32,128]{2,1,0:T(8,128)} async-done(((f32[2,32,128]{2,1,0:T(8,128)}), f32[128,32,128]{2,1,0:T(8,128)}) %all-gather.3.cloned.1.call-update) | async-done | bytes 2097168 | tf_op jit(solution)/shard_map/all_gather | solution.py:34
  155.3 2.2 gather_fusion
  157.5 1.2 fusion.4
  158.7 0.6 copy.46
  159.3 0.7 copy.50
  160.0 11.5 %all-to-all-start = ((s32[64,1,1]{2,1,0:T(1,128)}), s32[64,1,1]{2,1,0:T(1,128)S(1)}, u32[]{:S(2)}, u32[]{:S(2)}) async-start(s32[64,1,1]{2,1,0:T(1,128)} %copy.50), calls=%async_computation.1 | async-start | bytes 65536 | tf_op jit(solution)/shard_map/all_to_all | solution.py:27
  171.9 124.6 %all-gather.5.cloned.1.call-done = f32[128,32,128]{2,1,0:T(8,128)} async-done(((f32[2,32,128]{2,1,0:T(8,128)}), f32[128,32,128]{2,1,0:T(8,128)}) %all-gather.5.cloned.1.call-update) | async-done | bytes 2097168 | tf_op jit(solution)/shard_map/all_gather | solution.py:34
  296.4 2.2 gather_fusion.1
  298.6 0.6 gather_fusion.2
  300.4 0.9 divide_convert_fusion
  301.3 0.3 fusion
  302.0 1.3 convolution_bitcast_fusion
  303.3 1.6 copy.53
  304.9 11.5 %all-to-all-start.1 = ((f32[64,32,128]{2,1,0:T(8,128)}), f32[64,32,128]{2,1,0:T(8,128)S(1)}, u32[]{:S(2)}, u32[]{:S(2)}) async-start(f32[64,32,128]{2,1,0:T(8,128)} %copy.53), calls=%async_computation.2 | async-start | bytes 2097152 | tf_op jit(solution)/shard_map/all_to_all | solution.py:68
  316.4 0.9 fusion.17
  317.4 1.2 reduce
  318.6 41.0 %reduce-scatter.2.cloned.1.call-done = f32[2,32,128]{2,1,0:T(8,128)} async-done(((f32[2,32,1024]{2,1,0:T(8,128)}), f32[2,32,128]{2,1,0:T(8,128)}) %reduce-scatter.2.cloned.1.call-update) | async-done | bytes 32784 | tf_op jit(solution)/shard_map/reduce_scatter | solution.py:57
  359.5 1.4 multiply_multiply_fusion
  360.9 0.5 all-to-all-done.1
  361.5 1.0 fusion.1
  362.5 0.6 copy.55
  (29 shorter events, 1.8 us)
Async XLA Ops:
  7.2 152.2 %copy-start.3 = (s32[1,64]{1,0:T(1,128)S(1)}, s32[1,64]{1,0:T(1,128)}, u32[]{:S(2)}) copy-start(s32[1,64]{1,0:T(1,128)} %param.13) | copy-start | bytes 772
  7.2 164.4 %copy-start.2 = (s32[2,32]{1,0:T(2,128)S(1)}, s32[2,32]{1,0:T(2,128)}, u32[]{:S(2)}) copy-start(s32[2,32]{1,0:T(2,128)} %param.16) | copy-start | bytes 772
  7.2 164.4 %copy-start.4 = (s32[2,32]{1,0:T(2,128)S(1)}, s32[2,32]{1,0:T(2,128)}, u32[]{:S(2)}) copy-start(s32[2,32]{1,0:T(2,128)} %param.17) | copy-start | bytes 772
  7.2 148.1 %all-gather.3.cloned.1.call-start = ((), (), s32[]{:S(2)}) async-start(), calls=%async_computation.3 | async-start | bytes 2129920 | tf_op jit(solution)/shard_map/all_gather | solution.py:34
  7.9 288.5 %all-gather.5.cloned.1.call-start = ((), (), s32[]{:S(2)}) async-start(), calls=%async_computation.4 | async-start | bytes 2129920 | tf_op jit(solution)/shard_map/all_gather | solution.py:34
  160.0 144.8 %all-to-all-start = ((s32[64,1,1]{2,1,0:T(1,128)}), s32[64,1,1]{2,1,0:T(1,128)S(1)}, u32[]{:S(2)}, u32[]{:S(2)}) async-start(s32[64,1,1]{2,1,0:T(1,128)} %copy.50), calls=%async_computation.1 | async-start | bytes 65536 | tf_op jit(solution)/shard_map/all_to_all | solution.py:27
  299.5 0.9 copy-start
  299.5 0.9 copy-start.1
  304.9 56.6 %all-to-all-start.1 = ((f32[64,32,128]{2,1,0:T(8,128)}), f32[64,32,128]{2,1,0:T(8,128)S(1)}, u32[]{:S(2)}, u32[]{:S(2)}) async-start(f32[64,32,128]{2,1,0:T(8,128)} %copy.53), calls=%async_computation.2 | async-start | bytes 2097152 | tf_op jit(solution)/shard_map/all_to_all | solution.py:68
  316.4 43.2 %reduce-scatter.2.cloned.1.call-start = ((), (), s32[]{:S(2)}) async-start(), calls=%async_computation.5 | async-start | bytes 294912 | tf_op jit(solution)/shard_map/reduce_scatter | solution.py:57
Sparse Core Ops, SparseCore 0:
  11.0 144.2 all-gather.2
  159.4 136.9 all-gather.4
  320.0 39.4 reduce-scatter.1
where the time goes:
time: 370 us
  waiting for transfers between devices  313 us (85%)
  starting transfers between devices  23.1 us (6%)
  between operations  13.9 us (4%)
  local copies, waits for them, and re-layouts  9.82 us (3%)
  matrix products  5.71 us (2%)
  other arithmetic  4.49 us (1%)
    all_gather x2, waiting for transfers between devices, fetch_blocks(): whole_layer = lax.all_gather(layer_vals, 'node', axis=0, tiled=True)  270 us
    reduce_scatter x1, waiting for transfers between devices, local(): lax.psum_scatter(partial_counts, 'dp', scatter_dimension=2, tiled=True)  41 us
    all_to_all x1, starting transfers between devices, local(): lax.all_to_all(prod_asks.reshape(owners, 1), 'node', split_axis=0, concat...  11.5 us
    all_to_all x1, starting transfers between devices, local(): lax.all_to_all(slot_flows, 'node', split_axis=0, concat_axis=0, tiled=True)  11.5 us
  transfers between devices with their start and end apart: 5, of which 4 were waited for; matrix products, arithmetic and copies ran while one was open for 4% of the time, Pallas kernels for 0%

commit v1 on v0

--- a/solution.py
+++ b/solution.py
@@ -31,7 +31,8 @@
     ask_rows = (leaf_asks[0], prod_asks[0])
 
     def fetch_blocks(layer_vals, which_ask):
-        whole_layer = lax.all_gather(layer_vals, "node", axis=0, tiled=True)
+        sent = jnp.stack([layer_vals] * lax.axis_size("node"))
+        whole_layer = jnp.concatenate(lax.all_to_all(sent, "node", 0, 0), axis=0)
         return whole_layer[slot_iota * block_count + ask_rows[which_ask]]
 
     leaf_slots = fetch_blocks(leaf_logp, 0)

time: 370 us -> 328 us (0.89)
  the two profiles are of different devices: /device:TPU:2 before, /device:TPU:24 now
where the time goes in v1:
time: 328 us
  waiting for transfers between devices  257 us (78%)
  starting transfers between devices  38 us (12%)
  between operations  14.2 us (4%)
  local copies, waits for them, and re-layouts  10 us (3%)
  matrix products  5.71 us (2%)
    all_to_all x2, waiting for transfers between devices, fetch_blocks(): whole_layer = jnp.concatenate(lax.all_to_all(sent, 'node', 0, 0), axis=0)  199 us
    reduce_scatter x1, waiting for transfers between devices, local(): lax.psum_scatter(partial_counts, 'dp', scatter_dimension=2, tiled=True)  37.9 us
    all_to_all x2, starting transfers between devices, fetch_blocks(): whole_layer = jnp.concatenate(lax.all_to_all(sent, 'node', 0, 0), axis=0)  24.7 us
    all_to_all x1, waiting for transfers between devices, local(): lax.all_to_all(slot_flows, 'node', split_axis=0, concat_axis=0, tiled=True)  12.4 us
    all_to_all x1, waiting for transfers between devices, local(): lax.all_to_all(prod_asks.reshape(owners, 1), 'node', split_axis=0, concat...  7.68 us
    all_to_all x1, starting transfers between devices, local(): lax.all_to_all(slot_flows, 'node', split_axis=0, concat_axis=0, tiled=True)  7.42 us
  transfers between devices with their start and end apart: 5, of which 5 were waited for; matrix products, arithmetic and copies ran while one was open for 3% of the time, Pallas kernels for 0%

profile of v1, /device:TPU:24, one launch (start us, length us, event | category | flops | bytes accessed | tf_op | source)
XLA Modules:
  0.0 327.8 jit_solution(11461770835301077281)
XLA Ops:
  7.2 2.4 stack.4
  9.5 18.7 %all-to-all-start = ((f32[64,2,32,128]{3,2,1,0:T(8,128)}), f32[64,2,32,128]{3,2,1,0:T(8,128)S(1)}, u32[]{:S(2)}, u32[]{:S(2)}) async-start(f32[64,2,32,128]{3,2,1,0:T(8,128)} %stack.4), calls=%async_computation | async-start | bytes 4194304 | tf_op jit(solution)/shard_map/all_to_all | solution.py:35
  28.4 100.1 %all-to-all-done = f32[64,2,32,128]{3,2,1,0:T(8,128)S(1)} async-done(((f32[64,2,32,128]{3,2,1,0:T(8,128)}), f32[64,2,32,128]{3,2,1,0:T(8,128)S(1)}, u32[]{:S(2)}, u32[]{:S(2)}) %all-to-all-start) | async-done | bytes 2097184 | tf_op jit(solution)/shard_map/all_to_all | solution.py:35
  128.5 0.6 gather_fusion
  129.1 1.2 fusion.4
  130.3 1.6 stack.5
  131.9 6.0 %all-to-all-start.1 = ((f32[64,2,32,128]{3,2,1,0:T(8,128)}), f32[64,2,32,128]{3,2,1,0:T(8,128)S(1)}, u32[]{:S(2)}, u32[]{:S(2)}) async-start(f32[64,2,32,128]{3,2,1,0:T(8,128)} %stack.5), calls=%async_computation.1 | async-start | bytes 4194304 | tf_op jit(solution)/shard_map/all_to_all | solution.py:35
  138.2 0.7 copy.50
  138.9 98.7 %all-to-all-done.1 = f32[64,2,32,128]{3,2,1,0:T(8,128)S(1)} async-done(((f32[64,2,32,128]{3,2,1,0:T(8,128)}), f32[64,2,32,128]{3,2,1,0:T(8,128)S(1)}, u32[]{:S(2)}, u32[]{:S(2)}) %all-to-all-start.1) | async-done | bytes 2097184 | tf_op jit(solution)/shard_map/all_to_all | solution.py:35
  237.6 5.8 %all-to-all-start.2 = ((s32[64,1,1]{2,1,0:T(1,128)}), s32[64,1,1]{2,1,0:T(1,128)S(1)}, u32[]{:S(2)}, u32[]{:S(2)}) async-start(s32[64,1,1]{2,1,0:T(1,128)} %copy.50), calls=%async_computation.3 | async-start | bytes 65536 | tf_op jit(solution)/shard_map/all_to_all | solution.py:27
  243.4 0.6 gather_fusion.1
  244.1 0.6 gather_fusion.2
  245.8 0.9 divide_convert_fusion
  247.4 1.3 convolution_bitcast_fusion
  248.8 1.6 copy.53
  250.3 7.7 %all-to-all-done.2 = s32[64,1,1]{2,1,0:T(1,128)S(1)} async-done(((s32[64,1,1]{2,1,0:T(1,128)}), s32[64,1,1]{2,1,0:T(1,128)S(1)}, u32[]{:S(2)}, u32[]{:S(2)}) %all-to-all-start.2) | async-done | bytes 288 | tf_op jit(solution)/shard_map/all_to_all | solution.py:27
  258.0 7.4 %all-to-all-start.3 = ((f32[64,32,128]{2,1,0:T(8,128)}), f32[64,32,128]{2,1,0:T(8,128)S(1)}, u32[]{:S(2)}, u32[]{:S(2)}) async-start(f32[64,32,128]{2,1,0:T(8,128)} %copy.53), calls=%async_computation.4 | async-start | bytes 2097152 | tf_op jit(solution)/shard_map/all_to_all | solution.py:69
  265.5 0.9 fusion.17
  266.4 1.2 reduce
  267.7 37.9 %reduce-scatter.2.cloned.1.call-done = f32[2,32,128]{2,1,0:T(8,128)} async-done(((f32[2,32,1024]{2,1,0:T(8,128)}), f32[2,32,128]{2,1,0:T(8,128)}) %reduce-scatter.2.cloned.1.call-update) | async-done | bytes 32784 | tf_op jit(solution)/shard_map/reduce_scatter | solution.py:58
  305.6 1.4 multiply_multiply_fusion
  307.0 12.4 %all-to-all-done.3 = f32[64,32,128]{2,1,0:T(8,128)S(1)} async-done(((f32[64,32,128]{2,1,0:T(8,128)}), f32[64,32,128]{2,1,0:T(8,128)S(1)}, u32[]{:S(2)}, u32[]{:S(2)}) %all-to-all-start.3) | async-done | bytes 1048608 | tf_op jit(solution)/shard_map/all_to_all | solution.py:69
  319.3 1.0 fusion.1
  320.4 0.6 copy.55
  (35 shorter events, 2.2 us)
Async XLA Ops:
  9.5 18.7 %copy-start.7 = (s32[1,64]{1,0:T(1,128)S(1)}, s32[1,64]{1,0:T(1,128)}, u32[]{:S(2)}) copy-start(s32[1,64]{1,0:T(1,128)} %param.12) | copy-start | bytes 772
  9.5 18.7 %copy-start.3 = (s32[2,8]{1,0:T(2,128)S(1)}, s32[2,8]{1,0:T(2,128)}, u32[]{:S(2)}) copy-start(s32[2,8]{1,0:T(2,128)} %param.15) | copy-start | bytes 196
  9.5 18.8 %copy-start.4 = (s32[2,8]{1,0:T(2,128)S(1)}, s32[2,8]{1,0:T(2,128)}, u32[]{:S(2)}) copy-start(s32[2,8]{1,0:T(2,128)} %param.14) | copy-start | bytes 196
  9.5 118.9 %all-to-all-start = ((f32[64,2,32,128]{3,2,1,0:T(8,128)}), f32[64,2,32,128]{3,2,1,0:T(8,128)S(1)}, u32[]{:S(2)}, u32[]{:S(2)}) async-start(f32[64,2,32,128]{3,2,1,0:T(8,128)} %stack.4), calls=%async_computation | async-start | bytes 4194304 | tf_op jit(solution)/shard_map/all_to_all | solution.py:35
  131.9 6.0 %copy-start.2 = (s32[2,32]{1,0:T(2,128)S(1)}, s32[2,32]{1,0:T(2,128)}, u32[]{:S(2)}) copy-start(s32[2,32]{1,0:T(2,128)} %param.16) | copy-start | bytes 772
  131.9 6.1 %copy-start.6 = (s32[2,32]{1,0:T(2,128)S(1)}, s32[2,32]{1,0:T(2,128)}, u32[]{:S(2)}) copy-start(s32[2,32]{1,0:T(2,128)} %param.17) | copy-start | bytes 772
  131.9 6.3 %copy-start.5 = (s32[1,64]{1,0:T(1,128)S(1)}, s32[1,64]{1,0:T(1,128)}, u32[]{:S(2)}) copy-start(s32[1,64]{1,0:T(1,128)} %param.13) | copy-start | bytes 772
  131.9 105.7 %all-to-all-start.1 = ((f32[64,2,32,128]{3,2,1,0:T(8,128)}), f32[64,2,32,128]{3,2,1,0:T(8,128)S(1)}, u32[]{:S(2)}, u32[]{:S(2)}) async-start(f32[64,2,32,128]{3,2,1,0:T(8,128)} %stack.5), calls=%async_computation.1 | async-start | bytes 4194304 | tf_op jit(solution)/shard_map/all_to_all | solution.py:35
  237.6 20.4 %all-to-all-start.2 = ((s32[64,1,1]{2,1,0:T(1,128)}), s32[64,1,1]{2,1,0:T(1,128)S(1)}, u32[]{:S(2)}, u32[]{:S(2)}) async-start(s32[64,1,1]{2,1,0:T(1,128)} %copy.50), calls=%async_computation.3 | async-start | bytes 65536 | tf_op jit(solution)/shard_map/all_to_all | solution.py:27
  244.9 0.9 copy-start
  244.9 0.9 copy-start.1
  258.0 61.3 %all-to-all-start.3 = ((f32[64,32,128]{2,1,0:T(8,128)}), f32[64,32,128]{2,1,0:T(8,128)S(1)}, u32[]{:S(2)}, u32[]{:S(2)}) async-start(f32[64,32,128]{2,1,0:T(8,128)} %copy.53), calls=%async_computation.4 | async-start | bytes 2097152 | tf_op jit(solution)/shard_map/all_to_all | solution.py:69
  265.4 40.1 %reduce-scatter.2.cloned.1.call-start = ((), (), s32[]{:S(2)}) async-start(), calls=%async_computation.5 | async-start | bytes 294912 | tf_op jit(solution)/shard_map/reduce_scatter | solution.py:58
Sparse Core Ops, SparseCore 0:
  269.1 36.4 reduce-scatter.1
